TPU v7x, 512 devices: a whole 4x8x8 slice. The times are simulated.
512 devices in a mesh: replica: 32 (over z, x_hi, core), fsdp: 16 (over x_lo, y).
Axes of the slice: x: 4 (x_hi: 2, x_lo: 2; x = x_hi * 2 + x_lo), y: 8, z: 8, core: 2. Of those that a mesh axis runs over, the one named last changes fastest.
Arguments:
- tokens: bfloat16 [81920, 4608], P(('replica', 'fsdp')), may hold values from -8 to 8
- gain: float32 [32, 4608], P('replica'), may hold values from -0.5 to 0.5
- key_weight: bfloat16 [32, 4608, 1024], P('replica', 'fsdp'), may hold values from -2 to 2
- key_cotangent: bfloat16 [81920, 1024], P(('replica', 'fsdp')), may hold values from -6 to 6
- local_fragment: bfloat16 [32, 64, 4608], P('replica', 'fsdp'), may hold values from -6 to 6
- global_fragment: float32 [64, 4608], P('fsdp'), may hold values from -6 to 6
- outer_momentum: float32 [64, 4608], P('fsdp'), may hold values from -3 to 3
Outputs:
- keys: bfloat16 [81920, 1024], P(('replica', 'fsdp'))
- grad_tokens: bfloat16 [81920, 4608], P(('replica', 'fsdp'))
- grad_key_weight: bfloat16 [32, 4608, 1024], P('replica', 'fsdp')
- grad_gain: float32 [32, 4608], P('replica')
- new_global: float32 [64, 4608], P('fsdp')
- new_momentum: float32 [64, 4608], P('fsdp')
All inputs are finite; a program needn't handle non-finite values.
Results may differ from a plain program's by a relative error of at most 0.0049.
Values may be sent and summed in bfloat16 or wider, within the bound.
A program may use at most 64 MiB of HBM per device.

v0:
```python
import jax
import jax.numpy as jnp
from jax import lax
from jax.sharding import PartitionSpec as P

eps = 1e-06


def on_device(
    tokens, gain, key_weight, key_cotangent, local_fragment, global_fragment, outer_momentum
):
    xf = tokens.astype(jnp.float32)
    rstd = lax.rsqrt(jnp.mean(xf * xf, axis=-1, keepdims=True) + eps)
    unit = xf * rstd
    scale = 1.0 + gain[0]
    normed = (unit * scale).astype(jnp.bfloat16)
    weights = key_weight[0]
    piece = lax.all_gather(weights, "fsdp", axis=0, tiled=True)
    key_total = jnp.dot(normed, piece, preferred_element_type=jnp.float32)
    block = lax.dot_general(
        key_cotangent, piece, (((1,), (1,)), ((), ())), preferred_element_type=jnp.float32
    )
    grad_normed = block
    key_total, grad_normed = (key_total, grad_normed)
    columns_all = lax.all_to_all(normed, "fsdp", split_axis=1, concat_axis=0, tiled=True)
    grad_weight = lax.dot_general(
        columns_all,
        lax.all_gather(key_cotangent, "fsdp", axis=0, tiled=True),
        (((0,), (0,)), ((), ())),
        preferred_element_type=jnp.float32,
    )
    grad_gain = lax.psum(jnp.sum(grad_normed * unit, axis=0), "fsdp")
    scaled = grad_normed * scale
    grad_rows = rstd * (scaled - unit * jnp.mean(scaled * unit, axis=-1, keepdims=True))
    replicas = lax.axis_size("replica")
    delta = global_fragment - local_fragment[0].astype(jnp.float32)
    average = lax.psum(delta, "replica") / replicas
    new_momentum = 0.9 * outer_momentum + average
    new_global = global_fragment - 0.7 * (average + 0.9 * new_momentum)
    return (
        key_total.astype(jnp.bfloat16),
        grad_rows.astype(jnp.bfloat16),
        grad_weight.astype(jnp.bfloat16)[None],
        grad_gain[None],
        new_global,
        new_momentum,
    )


def solution(mesh):
    placed = (
        P(("replica", "fsdp"), None),
        P("replica", None),
        P("replica", "fsdp", None),
        P(("replica", "fsdp"), None),
        P("replica", "fsdp", None),
        P("fsdp", None),
        P("fsdp", None),
    )
    return jax.shard_map(
        on_device,
        mesh=mesh,
        in_specs=placed,
        out_specs=(
            P(("replica", "fsdp"), None),
            P(("replica", "fsdp"), None),
            P("replica", "fsdp", None),
            P("replica", None),
            P("fsdp", None),
            P("fsdp", None),
        ),
        check_vma=False,
    )
```

profile of v0, /device:TPU:6, one launch (start us, length us, event | category | flops | bytes accessed | tf_op | source)
XLA Modules:
  0.0 427.9 jit_solution(18060307562654005462)
XLA Ops:
  8.0 0.0 all-gather.6.cloned.1.call-start
  8.0 0.7 all-gather.6.cloned.1.call-update
  8.7 0.0 all-reduce.2.cloned.1.call-start
  8.8 1.5 convert_subtract_fusion
  10.3 0.0 all-reduce.2.cloned.1.call-update
  10.3 0.0 all-gather.4.cloned.1.call-start
  10.4 0.7 all-gather.4.cloned.1.call-update
  11.1 0.8 add_reduce_fusion
  11.9 1.8 fusion.14
  13.6 0.0 copy-start
  13.7 115.4 %all-gather.6.cloned.1.call-done = bf16[1,4608,1024]{2,1,0:T(8,128)(2,1)} async-done(((bf16[1,288,1024]{2,1,0:T(8,128)(2,1)}), bf16[1,4608,1024]{2,1,0:T(8,128)(2,1)}) %all-gather.6.cloned.1.call-update) | async-done | bytes 9437200 | tf_op jit(solution)/shard_map/all_gather | solution.py:18
  129.1 7.8 %fusion.13 = (f32[4608]{0:T(1024)S(1)}, f32[160]{0:T(256)S(1)}, f32[160,4608]{1,0:T(8,128)S(1)}) fusion(bf16[160,4608]{1,0:T(8,128)(2,1)} %param.7, f32[160]{0:T(256)S(1)} %add_rsqrt_fusion, f32[4608]{0:T(1024)S(1)} %add_reduce_fusion, bf16[160,1024]{1,0:T(8,128)(2,1)} %param.10, bf16[1,4608,1024]{2,1,0:T(8,128)(2,1)} %all-gather.6.cloned.1.call-done), kind=kOutput, calls=%fused_computation.15 | convolution fusion | flops 1515105664 | bytes 14226688 | tf_op jit(solution)/shard_map/dot_general | solution.py:20
  136.9 0.0 copy-done
  136.9 2.1 fusion.12
  139.0 2.7 all_to_all.14
  141.7 1.7 copy.13
  143.4 0.0 copy-start.1
  143.4 5.5 %all-to-all-start = ((bf16[160,16,288]{2,0,1:T(8,128)(2,1)}), bf16[160,16,288]{2,0,1:T(8,128)(2,1)S(1)}, u32[]{:S(2)}, u32[]{:S(2)}) async-start(bf16[160,16,288]{2,0,1:T(8,128)(2,1)} %copy.13), calls=%async_computation | async-start | bytes 3932160 | tf_op jit(solution)/shard_map/all_to_all | solution.py:25
  148.9 196.2 %all-reduce.2.cloned.1.call-done = f32[4,4608]{1,0:T(4,128)} async-done(((f32[4,4608]{1,0:T(4,128)}), f32[4,4608]{1,0:T(4,128)}) %all-reduce.2.cloned.1.call-update) | async-done | bytes 73744 | tf_op jit(solution)/shard_map/psum | solution.py:37
  345.1 0.0 copy-done.1
  345.1 1.6 multiply_subtract_fusion
  346.8 62.6 %psum.14 = f32[1,4608]{1,0:T(1,128)} all-reduce(f32[1,4608]{1,0:T(1,128)S(1)} %broadcast_in_dim.5), channel_id=1, replica_groups=mesh['replica'=32,'fsdp'=16] {'fsdp'}, use_global_device_ids=true, to_apply=%region_3.0 | all-reduce | flops 4608 | bytes 36864 | tf_op jit(solution)/shard_map/psum | solution.py:32
  409.4 6.1 %fusion.16 = bf16[160,1024]{1,0:T(8,128)(2,1)} fusion(bf16[160,4608]{1,0:T(8,128)(2,1)S(1)} %get-tuple-element.11, bf16[1,4608,1024]{2,1,0:T(8,128)(2,1)} %all-gather.6.cloned.1.call-done), kind=kOutput, calls=%fused_computation.19 | convolution fusion | flops 1510113280 | bytes 11239424 | tf_op jit(solution)/shard_map/dot_general | solution.py:19
  415.5 0.0 all-gather.4.cloned.1.call-done
  415.5 0.0 all-to-all-done
  415.5 5.0 %fusion.15 = bf16[1,288,1024]{2,1,0:T(8,128)(2,1)} fusion(bf16[2560,288]{1,0:T(8,128)(2,1)S(1)} %bitcast.21, bf16[2560,1024]{1,0:T(8,128)(2,1)} %all-gather.4.cloned.1.call-done), kind=kOutput, calls=%fused_computation.18 | convolution fusion | flops 1510244352 | bytes 7307264 | tf_op jit(solution)/shard_map/dot_general | solution.py:26
  (3 shorter events, 0.0 us)
Async XLA Ops:
  8.0 121.1 %all-gather.6.cloned.1.call-start = ((), (), s32[]{:S(2)}) async-start(), calls=%async_computation.3 | async-start | bytes 10027008 | tf_op jit(solution)/shard_map/all_gather | solution.py:18
  8.7 336.4 %all-reduce.2.cloned.1.call-start = ((), (), s32[]{:S(2)}) async-start(), calls=%async_computation.2 | async-start | bytes 147456 | tf_op jit(solution)/shard_map/psum | solution.py:37
  10.3 405.1 %all-gather.4.cloned.1.call-start = ((), (), s32[]{:S(2)}) async-start(), calls=%async_computation.1 | async-start | bytes 5570560 | tf_op jit(solution)/shard_map/all_gather | solution.py:28
  13.6 123.2 %copy-start = (bf16[160,4608]{1,0:T(8,128)(2,1)S(1)}, bf16[160,4608]{1,0:T(8,128)(2,1)}, u32[]{:S(2)}) copy-start(bf16[160,4608]{1,0:T(8,128)(2,1)} %param.7) | copy-start | bytes 4423684
  143.4 201.7 %copy-start.1 = (f32[4,4608]{1,0:T(4,128)S(1)}, f32[4,4608]{1,0:T(4,128)}, u32[]{:S(2)}) copy-start(f32[4,4608]{1,0:T(4,128)} %param.12) | copy-start | bytes 221188
  143.4 272.1 %all-to-all-start = ((bf16[160,16,288]{2,0,1:T(8,128)(2,1)}), bf16[160,16,288]{2,0,1:T(8,128)(2,1)S(1)}, u32[]{:S(2)}, u32[]{:S(2)}) async-start(bf16[160,16,288]{2,0,1:T(8,128)(2,1)} %copy.13), calls=%async_computation | async-start | bytes 3932160 | tf_op jit(solution)/shard_map/all_to_all | solution.py:25
Sparse Core Ops, SparseCore 0:
  10.9 118.1 all-gather.5
  131.1 118.2 all-gather.3
Sparse Core Ops, SparseCore 1:
  12.7 332.4 all-reduce.1
where the time goes:
time: 431 us; the launch traced here: 428 us
  waiting for transfers between devices  313 us (73%)
  blocking collectives  62.6 us (15%)
  matrix products  18.9 us (4%)
  between operations  15.5 us (4%)
  other arithmetic  7.81 us (2%)
  starting transfers between devices  5.61 us (1%)
  local copies, waits for them, and re-layouts  4.44 us (1%)
    psum x1, waiting for transfers between devices, on_device(): average = lax.psum(delta, 'replica') / replicas  196 us
    all_gather x1, waiting for transfers between devices, on_device(): piece = lax.all_gather(weights, 'fsdp', axis=0, tiled=True)  115 us
    psum x1, blocking collectives, on_device(): grad_gain = lax.psum(jnp.sum(grad_normed * unit, axis=0), 'fsdp')  62.6 us
  transfers between devices with their start and end apart: 4, of which 2 were waited for; matrix products, arithmetic and copies ran while one was open for 5% of the time, Pallas kernels for 0%

commit v1 on v0

v1 whole, which is shorter than its diff:
```python
import functools

import jax
import jax.numpy as jnp
from jax import lax
from jax.experimental import pallas as pl
from jax.experimental.pallas import tpu as pltpu
from jax.sharding import PartitionSpec as P

eps = 1e-06
MESH = pl.DeviceIdType.MESH
f32, bf16 = jnp.float32, jnp.bfloat16

RING = 8
ROWS = 160
D = 4608
HALF = D // 2
KV = 1024
SHARD = 288
PIECE = SHARD // 2
HOPS = 7


def kernel(
    tok, gain, w, cot, frag, glob, mom,
    keys_o, gtok_o, gw_o, ggain_o, nglob_o, nmom_o,
    tokv, gainv, n2, nsend, c2, wall, part, rs_s, rs_r, dn_own, dn_s, dn_r, k_own, k_s, k_r,
    rstdv, gtokv, keysv, gwv, fragv, globv, momv, nglobv, nmomv,
    zring, zsum, core_r, csum, xhi_r, gring, gsum, gx_r, ggainv,
    ag_ss, ag_rs, rs_ss, rs_rs, x_ss, x_rs, z_ss, z_rs, g_ss, g_rs, h_ss, h_rs, loc,
):
    me = lax.axis_index("fsdp")
    rep = lax.axis_index("replica")
    x, y = me // RING, me % RING
    z, low = rep // 4, rep % 4
    core, xhi = low % 2, low // 2

    def fs(i):
        return {"fsdp": i}

    def rp(i):
        return {"replica": i}

    ring = (fs(x * RING + (y + 1) % RING), fs(x * RING + (y + RING - 1) % RING))
    zring_dev = (rp((z + 1) % RING * 4 + low), rp((z + RING - 1) % RING * 4 + low))
    partner = fs((1 - x) * RING + y)
    core_dev = rp(rep + 1 - 2 * core)
    xhi_dev = rp(rep + 2 - 4 * xhi)

    def local(i, src, dst):
        return pltpu.make_async_copy(src, dst, loc.at[i])

    def remote(src, dst, ss, rs, dev):
        return pltpu.make_async_remote_copy(
            src_ref=src, dst_ref=dst, send_sem=ss, recv_sem=rs, device_id=dev, device_id_type=MESH
        )

    own_rows = pl.ds(pl.multiple_of(y * SHARD, 16), SHARD)
    loads = [
        local(0, frag.at[0], fragv),
        local(1, tok, tokv),
        local(2, gain, gainv),
        local(3, cot, c2.at[pl.ds(0, ROWS)]),
        local(4, w.at[0], wall.at[own_rows]),
        local(5, glob, globv),
        local(6, mom, momv),
    ]
    for copy in loads:
        copy.start()

    barrier = pltpu.get_barrier_semaphore()
    peers = ring + zring_dev + (partner, core_dev, xhi_dev)
    for peer in peers:
        pl.semaphore_signal(barrier, inc=1, device_id=peer, device_id_type=MESH)
    pl.semaphore_wait(barrier, len(peers))

    def wpiece(direction, j, extra):
        away = j // 2 + extra
        shard = (y + RING - away) % RING if direction == 0 else (y + away) % RING
        half = (j % 2) ^ direction
        return wall.at[pl.ds(pl.multiple_of(shard * SHARD + half * PIECE, 16), PIECE)]

    def ag_copy(direction, j):
        there = wpiece(direction, j, 0)
        half = (j % 2) ^ direction
        src = w.at[0, pl.ds(half * PIECE, PIECE)] if j < 2 else there
        return remote(src, there, ag_ss.at[direction, j], ag_rs.at[direction, j], ring[direction])

    def ag_arrive(j):
        for direction in (0, 1):
            here = wpiece(direction, j, 1)
            remote(
                here, here, ag_ss.at[direction, j], ag_rs.at[direction, j], ring[direction]
            ).wait_recv()
            if j + 2 < HOPS:
                ag_copy(direction, j + 2).start()

    for j in (0, 1):
        for direction in (0, 1):
            ag_copy(direction, j).start()

    x_c = remote(cot, c2.at[pl.ds(ROWS, ROWS)], x_ss.at[0], x_rs.at[0], partner)
    x_n = remote(nsend, n2.at[pl.ds(ROWS, ROWS)], x_ss.at[1], x_rs.at[1], partner)
    x_dn = remote(dn_s, dn_r, x_ss.at[2], x_rs.at[2], partner)
    x_k = remote(k_s, k_r, x_ss.at[3], x_rs.at[3], partner)
    x_g = remote(gsum, gx_r, x_ss.at[4], x_rs.at[4], partner)
    x_c.start()

    def small_ring(buf, at, ss, rs, devs):
        def slot(direction, hop):
            return buf.at[(at + RING - hop) % RING if direction == 0 else (at + hop) % RING]

        def send(direction, hop):
            return remote(
                slot(direction, hop), slot(direction, hop),
                ss.at[direction, hop], rs.at[direction, hop], devs[direction],
            )

        def arrive(hop):
            for direction in (0, 1):
                if hop < 4 - direction:
                    here = slot(direction, hop + 1)
                    remote(
                        here, here, ss.at[direction, hop], rs.at[direction, hop], devs[direction]
                    ).wait_recv()
                    if hop + 1 < 4 - direction:
                        send(direction, hop + 1).start()

        return send, arrive

    z_send, z_arrive = small_ring(zring, z, z_ss, z_rs, zring_dev)
    g_send, g_arrive = small_ring(gring, y, g_ss, g_rs, ring)

    loads[0].wait()
    zring[z, pl.ds(0, 4)] = fragv[:, pl.ds(0, HALF)].astype(f32)
    zring[z, pl.ds(4, 4)] = fragv[:, pl.ds(HALF, HALF)].astype(f32)
    z_send(0, 0).start()
    z_send(1, 0).start()

    loads[1].wait()
    loads[2].wait()
    mine = x * HALF
    other = (1 - x) * HALF
    step = 768

    def cols(base, at):
        return pl.ds(pl.multiple_of(base + at, 128), step)

    def norm_block(i, _):
        rows = pl.ds(pl.multiple_of(i * 16, 16), 16)
        total = jnp.zeros((16, 128), f32)
        for at in range(0, D, step):
            v = tokv[rows, pl.ds(at, step)].astype(f32)
            v = v * v
            for k in range(0, step, 128):
                total = total + v[:, k : k + 128]
        mean = jnp.sum(total, axis=-1, keepdims=True) * (1.0 / D)
        rstd = lax.rsqrt(mean + eps)
        rstdv[rows, :] = jnp.broadcast_to(rstd, (16, 128))
        for base, to in ((other, nsend), (mine, n2)):
            for at in range(0, HALF, step):
                unit = tokv[rows, cols(base, at)].astype(f32) * rstd
                to[rows, pl.ds(at, step)] = (unit * (1.0 + gainv[:, cols(base, at)])).astype(bf16)
        return 0

    lax.fori_loop(0, ROWS // 16, norm_block, 0)
    x_n.start()

    ag_arrive(0)
    z_arrive(0)
    ag_arrive(1)
    z_arrive(1)
    ag_arrive(2)
    z_arrive(2)
    ag_arrive(3)
    z_arrive(3)

    loads[3].wait()
    x_c.wait_recv()
    x_n.wait_recv()

    def part_block(i, _):
        at = pl.multiple_of(i * 256, 256)
        part[pl.ds(at, 256), :] = lax.dot_general(
            n2[:, pl.ds(at, 256)], c2[...], (((0,), (0,)), ((), ())), preferred_element_type=f32
        )
        return 0

    lax.fori_loop(0, HALF // 256, part_block, 0)

    ag_arrive(4)

    def part_rows(direction, away, half, i):
        shard = (y + away) % RING if direction == 0 else (y + RING - away) % RING
        return pl.ds(pl.multiple_of(shard * SHARD + half * PIECE + i * 16, 16), 16)

    def rs_copy(direction, j):
        return remote(
            rs_s.at[direction, j], rs_r.at[direction, j],
            rs_ss.at[direction, j], rs_rs.at[direction, j], ring[direction],
        )

    def rs_send(direction, j):
        half, away = (j % 2) ^ direction, 4 - (j + 1) // 2

        def block(i, _):
            rows = pl.ds(pl.multiple_of(i * 16, 16), 16)
            v = part[part_rows(direction, away, half, i), :]
            if j >= 2:
                v = v + rs_r[direction, j - 2, rows, :].astype(f32)
            rs_s[direction, j, rows, :] = v.astype(bf16)
            return 0

        lax.fori_loop(0, PIECE // 16, block, 0)
        rs_copy(direction, j).start()

    def rs_arrive(j):
        for direction in (0, 1):
            rs_copy(direction, j).wait_recv()
            if j + 2 < HOPS:
                rs_send(direction, j + 2)

    for j in (0, 1):
        for direction in (0, 1):
            rs_send(direction, j)

    total = zring[0]
    for k in range(1, RING):
        total = total + zring[k]
    zsum[...] = total
    x_core = remote(zsum, core_r, h_ss.at[0], h_rs.at[0], core_dev)
    x_xhi = remote(csum, xhi_r, h_ss.at[1], h_rs.at[1], xhi_dev)
    x_core.start()

    ag_arrive(5)
    x_core.wait_recv()
    csum[...] = zsum[...] + core_r[...]
    x_xhi.start()
    ag_arrive(6)
    loads[4].wait()

    def dn_block(i, _):
        at = pl.multiple_of(i * 256, 256)
        v = lax.dot_general(
            c2[...], wall[pl.ds(at, 256), :], (((1,), (1,)), ((), ())), preferred_element_type=f32
        )
        dn_own[:, pl.ds(at, 256)] = v[:ROWS]
        dn_s[:, pl.ds(at, 256)] = v[ROWS:].astype(bf16)
        gring[y, :, pl.ds(at, 256)] = jnp.sum(
            v * n2[:, pl.ds(at, 256)].astype(f32), axis=0, keepdims=True
        )
        return 0

    lax.fori_loop(0, HALF // 256, dn_block, 0)
    x_dn.start()
    g_send(0, 0).start()
    g_send(1, 0).start()

    def key_block(i, _):
        at = pl.multiple_of(i * 256, 256)
        v = jnp.dot(n2[...], wall[:, pl.ds(at, 256)], preferred_element_type=f32)
        k_own[:, pl.ds(at, 256)] = v[:ROWS]
        k_s[:, pl.ds(at, 256)] = v[ROWS:].astype(bf16)
        return 0

    lax.fori_loop(0, KV // 256, key_block, 0)
    x_k.start()

    rs_arrive(0)
    g_arrive(0)

    loads[5].wait()
    loads[6].wait()
    x_xhi.wait_recv()
    for k in (0, 1):
        here = pl.ds(k * HALF, HALF)
        locals_sum = csum[pl.ds(4 * k, 4), :] + xhi_r[pl.ds(4 * k, 4), :]
        g = globv[:, here]
        average = (32.0 * g - locals_sum) * (1.0 / 32.0)
        momentum = 0.9 * momv[:, here] + average
        nmomv[:, here] = momentum
        nglobv[:, here] = g - 0.7 * (average + 0.9 * momentum)
    stores = [local(7, nglobv, nglob_o), local(8, nmomv, nmom_o)]
    for copy in stores:
        copy.start()

    rs_arrive(1)
    g_arrive(1)
    rs_arrive(2)
    g_arrive(2)
    rs_arrive(3)
    g_arrive(3)

    total = gring[0]
    for k in range(1, RING):
        total = total + gring[k]
    gsum[...] = total / (1.0 + gainv[:, pl.ds(pl.multiple_of(mine, 128), HALF)])
    x_g.start()

    x_k.wait_recv()

    def keys_block(i, _):
        rows = pl.ds(pl.multiple_of(i * 16, 16), 16)
        keysv[rows, :] = (k_own[rows, :] + k_r[rows, :].astype(f32)).astype(bf16)
        return 0

    lax.fori_loop(0, ROWS // 16, keys_block, 0)
    store = local(9, keysv, keys_o)
    store.start()
    stores.append(store)

    x_dn.wait_recv()
    rs_arrive(4)

    def gtok_block(i, _):
        rows = pl.ds(pl.multiple_of(i * 16, 16), 16)
        rstd = rstdv[rows, pl.ds(0, 1)]
        total = jnp.zeros((16, 128), f32)
        for base, grad in ((mine, dn_own), (other, dn_r)):
            for at in range(0, HALF, step):
                unit = tokv[rows, cols(base, at)].astype(f32) * rstd
                scaled = grad[rows, pl.ds(at, step)].astype(f32) * (1.0 + gainv[:, cols(base, at)])
                v = scaled * unit
                for k in range(0, step, 128):
                    total = total + v[:, k : k + 128]
        mean = jnp.sum(total, axis=-1, keepdims=True) * (1.0 / D)
        for base, grad in ((mine, dn_own), (other, dn_r)):
            for at in range(0, HALF, step):
                unit = tokv[rows, cols(base, at)].astype(f32) * rstd
                scaled = grad[rows, pl.ds(at, step)].astype(f32) * (1.0 + gainv[:, cols(base, at)])
                gtokv[rows, cols(base, at)] = (rstd * (scaled - unit * mean)).astype(bf16)
        return 0

    lax.fori_loop(0, ROWS // 16, gtok_block, 0)
    store = local(10, gtokv, gtok_o)
    store.start()
    stores.append(store)

    x_g.wait_recv()
    ggainv[:, pl.ds(pl.multiple_of(mine, 128), HALF)] = gsum[...]
    ggainv[:, pl.ds(pl.multiple_of(other, 128), HALF)] = gx_r[...]
    store = local(11, ggainv, ggain_o)
    store.start()
    stores.append(store)

    rs_arrive(5)

    def early_block(direction):
        half = 1 - direction

        def block(i, _):
            rows = part_rows(0, 0, half, i)
            arrived = rs_r[direction, 5, pl.ds(pl.multiple_of(i * 16, 16), 16), :]
            part[rows, :] = part[rows, :] + arrived.astype(f32)
            return 0

        return block

    for direction in (0, 1):
        lax.fori_loop(0, PIECE // 16, early_block(direction), 0)
    rs_arrive(6)

    def last_block(direction):
        half = direction

        def block(i, _):
            arrived = rs_r[direction, 6, pl.ds(pl.multiple_of(i * 16, 16), 16), :]
            to = pl.ds(pl.multiple_of(half * PIECE + i * 16, 16), 16)
            v = part[part_rows(0, 0, half, i), :] + arrived.astype(f32)
            gwv[to, :] = v.astype(bf16)
            return 0

        return block

    for direction in (0, 1):
        lax.fori_loop(0, PIECE // 16, last_block(direction), 0)
    store = local(12, gwv, gw_o.at[0])
    store.start()
    stores.append(store)

    for direction in (0, 1):
        for j in range(HOPS):
            ag_copy(direction, j).wait_send()
            rs_copy(direction, j).wait_send()
        for hop in range(4 - direction):
            z_send(direction, hop).wait_send()
            g_send(direction, hop).wait_send()
    for copy in (x_c, x_n, x_dn, x_k, x_g, x_core, x_xhi):
        copy.wait_send()
    for copy in stores:
        copy.wait()


def on_device(tokens, gain, key_weight, key_cotangent, local_fragment, global_fragment, outer_momentum):
    v, dma = pltpu.VMEM, pltpu.SemaphoreType.DMA
    return pl.pallas_call(
        kernel,
        out_shape=(
            jax.ShapeDtypeStruct((ROWS, KV), bf16),
            jax.ShapeDtypeStruct((ROWS, D), bf16),
            jax.ShapeDtypeStruct((1, SHARD, KV), bf16),
            jax.ShapeDtypeStruct((1, D), f32),
            jax.ShapeDtypeStruct((4, D), f32),
            jax.ShapeDtypeStruct((4, D), f32),
        ),
        in_specs=[pl.BlockSpec(memory_space=pl.ANY)] * 7,
        out_specs=[pl.BlockSpec(memory_space=pl.ANY)] * 6,
        scratch_shapes=[
            v((ROWS, D), bf16),
            v((1, D), f32),
            v((2 * ROWS, HALF), bf16),
            v((ROWS, HALF), bf16),
            v((2 * ROWS, KV), bf16),
            v((HALF, KV), bf16),
            v((HALF, KV), f32),
            v((2, HOPS, PIECE, KV), bf16),
            v((2, HOPS, PIECE, KV), bf16),
            v((ROWS, HALF), f32),
            v((ROWS, HALF), bf16),
            v((ROWS, HALF), bf16),
            v((ROWS, KV), f32),
            v((ROWS, KV), bf16),
            v((ROWS, KV), bf16),
            v((ROWS, 128), f32),
            v((ROWS, D), bf16),
            v((ROWS, KV), bf16),
            v((SHARD, KV), bf16),
            v((4, D), bf16),
            v((4, D), f32),
            v((4, D), f32),
            v((4, D), f32),
            v((4, D), f32),
            v((RING, 8, HALF), f32),
            v((8, HALF), f32),
            v((8, HALF), f32),
            v((8, HALF), f32),
            v((8, HALF), f32),
            v((RING, 1, HALF), f32),
            v((1, HALF), f32),
            v((1, HALF), f32),
            v((1, D), f32),
            dma((2, HOPS)),
            dma((2, HOPS)),
            dma((2, HOPS)),
            dma((2, HOPS)),
            dma((5,)),
            dma((5,)),
            dma((2, 4)),
            dma((2, 4)),
            dma((2, 4)),
            dma((2, 4)),
            dma((2,)),
            dma((2,)),
            dma((13,)),
        ],
        compiler_params=pltpu.CompilerParams(
            collective_id=0, has_side_effects=True, vmem_limit_bytes=52 * 2**20
        ),
        cost_estimate=pl.CostEstimate(
            flops=6 * ROWS * D * KV, bytes_accessed=8 * 2**20, transcendentals=ROWS
        ),
    )(tokens, gain, key_weight, key_cotangent, local_fragment, global_fragment, outer_momentum)


def solution(mesh):
    placed = (
        P(("replica", "fsdp"), None),
        P("replica", None),
        P("replica", "fsdp", None),
        P(("replica", "fsdp"), None),
        P("replica", "fsdp", None),
        P("fsdp", None),
        P("fsdp", None),
    )
    return jax.shard_map(
        on_device,
        mesh=mesh,
        in_specs=placed,
        out_specs=(
            P(("replica", "fsdp"), None),
            P(("replica", "fsdp"), None),
            P("replica", "fsdp", None),
            P("replica", None),
            P("fsdp", None),
            P("fsdp", None),
        ),
        check_vma=False,
    )
```

time: 431 us -> 116 us (0.27)
  waiting for transfers between devices: 313 us -> 0 us
  Pallas kernels: 0 us -> 105 us
  blocking collectives: 62.6 us -> 0 us
  matrix products: 18.9 us -> 0 us
  between operations: 15.5 us -> 0.66 us
  other arithmetic: 7.81 us -> 0 us
  local copies, waits for them, and re-layouts: 4.44 us -> 10.2 us
  starting transfers between devices: 5.61 us -> 0 us
    psum x1 -> x0, waiting for transfers between devices: 196 us -> none  [on_device(): average = lax.psum(delta, 'replica') / replicas]
    all_gather x2 -> x0, waiting for transfers between devices: 115 us -> none  [the longest x1 115 us: on_device(): piece = lax.all_gather(weights, 'fsdp', axis=0, tiled=True)]
    pallas_call x0 -> x1, Pallas kernels: none -> 105 us  [on_device(): pl.pallas_call(kernel, out_shape=(jax.ShapeDtypeStruct((ROWS, KV), bf16),...]
    psum x1 -> x0, blocking collectives: 62.6 us -> none  [on_device(): grad_gain = lax.psum(jnp.sum(grad_normed * unit, axis=0), 'fsdp')]
    dot_general x3 -> x0, matrix products: 18.9 us -> none  [the longest x1 7.77 us: on_device(): lax.dot_general(key_cotangent, piece, (((1,), (1,)), ((), ())), preferred...]
    unnamed x4 -> x16, local copies, waits for them, and re-layouts: 0.01 us -> 10.2 us
    all_to_all x1 -> x0, starting transfers between devices: 5.49 us -> none  [on_device(): lax.all_to_all(normed, 'fsdp', split_axis=1, concat_axis=0, tiled=True)]
    all_to_all x2 -> x0, local copies, waits for them, and re-layouts: 4.42 us -> none  [on_device(): lax.all_to_all(normed, 'fsdp', split_axis=1, concat_axis=0, tiled=True)]
  transfers between devices with their start and end apart: 4 -> 0, of which waited for: 2 -> 0; matrix products, arithmetic and copies ran while one was open for 5% -> 0% of each run, Pallas kernels for 0% -> 0%
where the time goes in v1:
time: 116 us
  Pallas kernels  105 us (91%)
  local copies, waits for them, and re-layouts  10.2 us (9%)
    pallas_call x1, Pallas kernels, on_device(): pl.pallas_call(kernel, out_shape=(jax.ShapeDtypeStruct((ROWS, KV), bf16),...  105 us
    unnamed x16, local copies, waits for them, and re-layouts  10.2 us

profile of v1, /device:TPU:6, one launch (start us, length us, event | category | flops | bytes accessed | tf_op | source)
XLA Modules:
  0.0 115.8 jit_solution(17009657740107593726)
XLA Ops:
  0.6 0.0 copy-start
  0.6 1.0 copy-done
  1.6 0.0 copy-start.1
  1.6 0.9 copy-done.1
  2.5 0.0 copy-start.2
  2.5 0.9 copy-done.2
  3.4 0.0 copy-start.3
  3.4 0.8 copy-done.3
  4.1 0.0 copy-start.4
  4.1 0.7 copy-done.4
  4.9 105.0 %shard_map.118 = (bf16[160,1024]{1,0:T(8,128)(2,1)S(1)}, bf16[160,4608]{1,0:T(8,128)(2,1)}, bf16[1,288,1024]{2,1,0:T(8,128)(2,1)S(1)}, f32[1,4608]{1,0:T(1,128)S...) custom-call(bf16[160,4608]{1,0:T(8,128)(2,1)} %tok.1, f32[1,4608]{1,0:T(1,128)S(1)} %copy-done.4, ...), custom_call_target="tpu_custom_call" | custom-call | flops 4529848320 | bytes 8388608 | tf_op jit(solution)/shard_map/pallas_call | solution.py:396
  109.8 0.7 copy.19
  110.6 2.6 %copy.20 = bf16[160,4608]{1,0:T(8,128)(2,1)} copy(bf16[160,4608]{1,0:T(8,128)(2,1)} %get-tuple-element.13) | data formatting | bytes 2949120
  113.1 0.8 copy.21
  114.0 0.6 copy.22
  114.6 0.6 copy.23
  115.2 0.6 copy.24
Async XLA Ops:
  0.6 1.0 copy-start
  1.6 0.9 copy-start.1
  2.5 0.9 copy-start.2
  3.4 0.8 copy-start.3
  4.1 0.7 copy-start.4

commit v2 on v1

--- a/solution.py
+++ b/solution.py
@@ -26,8 +26,8 @@
     keys_o, gtok_o, gw_o, ggain_o, nglob_o, nmom_o,
     tokv, gainv, n2, nsend, c2, wall, part, rs_s, rs_r, dn_own, dn_s, dn_r, k_own, k_s, k_r,
     rstdv, gtokv, keysv, gwv, fragv, globv, momv, nglobv, nmomv,
-    zring, zsum, core_r, csum, xhi_r, gring, gsum, gx_r, ggainv,
-    ag_ss, ag_rs, rs_ss, rs_rs, x_ss, x_rs, z_ss, z_rs, g_ss, g_rs, h_ss, h_rs, loc,
+    zacc, zin_r, core_r, csum, xhi_r, ztotal, gring, gsum, gx_r, ggainv,
+    ag_ss, ag_rs, rs_ss, rs_rs, x_ss, x_rs, z_ss, z_rs, g_ss, g_rs, above_in, loc,
 ):
     me = lax.axis_index("fsdp")
     rep = lax.axis_index("replica")
@@ -42,7 +42,8 @@
         return {"replica": i}
 
     ring = (fs(x * RING + (y + 1) % RING), fs(x * RING + (y + RING - 1) % RING))
-    zring_dev = (rp((z + 1) % RING * 4 + low), rp((z + RING - 1) % RING * 4 + low))
+    last = RING - 1
+    above, below = rp((z + 1) % RING * 4 + low), rp((z + last) % RING * 4 + low)
     partner = fs((1 - x) * RING + y)
     core_dev = rp(rep + 1 - 2 * core)
     xhi_dev = rp(rep + 2 - 4 * xhi)
@@ -69,10 +70,28 @@
         copy.start()
 
     barrier = pltpu.get_barrier_semaphore()
-    peers = ring + zring_dev + (partner, core_dev, xhi_dev)
-    for peer in peers:
+
+    def greet(peer):
         pl.semaphore_signal(barrier, inc=1, device_id=peer, device_id_type=MESH)
-    pl.semaphore_wait(barrier, len(peers))
+
+    for peer in ring + (partner,):
+        greet(peer)
+
+    @pl.when(z < last)
+    def _():
+        greet(above)
+
+    @pl.when(z == last)
+    def _():
+        greet(core_dev)
+        greet(xhi_dev)
+
+    greeted = 3 + jnp.where(z > 0, 1, 0) + jnp.where(z == last, 2, 0)
+    pl.semaphore_wait(barrier, greeted)
+
+    @pl.when(z > 0)
+    def _():
+        pl.semaphore_signal(above_in, inc=1, device_id=below, device_id_type=MESH)
 
     def wpiece(direction, j, extra):
         away = j // 2 + extra
@@ -99,11 +118,12 @@
         for direction in (0, 1):
             ag_copy(direction, j).start()
 
-    x_c = remote(cot, c2.at[pl.ds(ROWS, ROWS)], x_ss.at[0], x_rs.at[0], partner)
+    x_c = remote(c2.at[pl.ds(0, ROWS)], c2.at[pl.ds(ROWS, ROWS)], x_ss.at[0], x_rs.at[0], partner)
     x_n = remote(nsend, n2.at[pl.ds(ROWS, ROWS)], x_ss.at[1], x_rs.at[1], partner)
     x_dn = remote(dn_s, dn_r, x_ss.at[2], x_rs.at[2], partner)
     x_k = remote(k_s, k_r, x_ss.at[3], x_rs.at[3], partner)
     x_g = remote(gsum, gx_r, x_ss.at[4], x_rs.at[4], partner)
+    loads[3].wait()
     x_c.start()
 
     def small_ring(buf, at, ss, rs, devs):
@@ -128,14 +148,53 @@
 
         return send, arrive
 
-    z_send, z_arrive = small_ring(zring, z, z_ss, z_rs, zring_dev)
     g_send, g_arrive = small_ring(gring, y, g_ss, g_rs, ring)
 
+    z_up = remote(zacc, zin_r, z_ss.at[0], z_rs.at[0], above)
+    z_core = remote(zacc, core_r, z_ss.at[1], z_rs.at[1], core_dev)
+    z_xhi = remote(csum, xhi_r, z_ss.at[2], z_rs.at[2], xhi_dev)
+    z_down = remote(ztotal, ztotal, z_ss.at[3], z_rs.at[3], below)
+
+    def z_rise(low, high):
+        @pl.when((z >= low) & (z <= high))
+        def _():
+            if low > 0:
+                z_up.wait_recv()
+                zacc[...] = zacc[...] + zin_r[...]
+            if high < last:
+                pl.semaphore_wait(above_in, 1)
+                z_up.start()
+
+        if high == last:
+
+            @pl.when(z == last)
+            def _():
+                z_core.start()
+
+    def z_turn_core():
+        @pl.when(z == last)
+        def _():
+            z_core.wait_recv()
+            csum[...] = zacc[...] + core_r[...]
+            z_xhi.start()
+
+    def z_turn_x():
+        @pl.when(z == last)
+        def _():
+            z_xhi.wait_recv()
+            ztotal[...] = csum[...] + xhi_r[...]
+            z_down.start()
+
+    def z_fall(at):
+        @pl.when(z == at)
+        def _():
+            z_down.wait_recv()
+            if at > 0:
+                z_down.start()
+
     loads[0].wait()
-    zring[z, pl.ds(0, 4)] = fragv[:, pl.ds(0, HALF)].astype(f32)
-    zring[z, pl.ds(4, 4)] = fragv[:, pl.ds(HALF, HALF)].astype(f32)
-    z_send(0, 0).start()
-    z_send(1, 0).start()
+    zacc[pl.ds(0, 4), :] = fragv[:, pl.ds(0, HALF)].astype(f32)
+    zacc[pl.ds(4, 4), :] = fragv[:, pl.ds(HALF, HALF)].astype(f32)
 
     loads[1].wait()
     loads[2].wait()
@@ -165,17 +224,18 @@
 
     lax.fori_loop(0, ROWS // 16, norm_block, 0)
     x_n.start()
+    z_rise(0, 0)
 
     ag_arrive(0)
-    z_arrive(0)
+    z_rise(1, 2)
     ag_arrive(1)
-    z_arrive(1)
+    z_rise(3, 4)
     ag_arrive(2)
-    z_arrive(2)
+    z_rise(5, 6)
+    z_rise(7, 7)
     ag_arrive(3)
-    z_arrive(3)
-
-    loads[3].wait()
+    z_turn_core()
+
     x_c.wait_recv()
     x_n.wait_recv()
 
@@ -189,6 +249,7 @@
     lax.fori_loop(0, HALF // 256, part_block, 0)
 
     ag_arrive(4)
+    z_turn_x()
 
     def part_rows(direction, away, half, i):
         shard = (y + away) % RING if direction == 0 else (y + RING - away) % RING
@@ -224,19 +285,10 @@
         for direction in (0, 1):
             rs_send(direction, j)
 
-    total = zring[0]
-    for k in range(1, RING):
-        total = total + zring[k]
-    zsum[...] = total
-    x_core = remote(zsum, core_r, h_ss.at[0], h_rs.at[0], core_dev)
-    x_xhi = remote(csum, xhi_r, h_ss.at[1], h_rs.at[1], xhi_dev)
-    x_core.start()
-
     ag_arrive(5)
-    x_core.wait_recv()
-    csum[...] = zsum[...] + core_r[...]
-    x_xhi.start()
+    z_fall(6)
     ag_arrive(6)
+    z_fall(5)
     loads[4].wait()
 
     def dn_block(i, _):
@@ -267,29 +319,20 @@
     x_k.start()
 
     rs_arrive(0)
+    z_fall(4)
     g_arrive(0)
 
-    loads[5].wait()
-    loads[6].wait()
-    x_xhi.wait_recv()
-    for k in (0, 1):
-        here = pl.ds(k * HALF, HALF)
-        locals_sum = csum[pl.ds(4 * k, 4), :] + xhi_r[pl.ds(4 * k, 4), :]
-        g = globv[:, here]
-        average = (32.0 * g - locals_sum) * (1.0 / 32.0)
-        momentum = 0.9 * momv[:, here] + average
-        nmomv[:, here] = momentum
-        nglobv[:, here] = g - 0.7 * (average + 0.9 * momentum)
-    stores = [local(7, nglobv, nglob_o), local(8, nmomv, nmom_o)]
-    for copy in stores:
-        copy.start()
-
     rs_arrive(1)
+    z_fall(3)
     g_arrive(1)
     rs_arrive(2)
+    z_fall(2)
     g_arrive(2)
     rs_arrive(3)
+    z_fall(1)
     g_arrive(3)
+
+    stores = []
 
     total = gring[0]
     for k in range(1, RING):
@@ -311,6 +354,7 @@
 
     x_dn.wait_recv()
     rs_arrive(4)
+    z_fall(0)
 
     def gtok_block(i, _):
         rows = pl.ds(pl.multiple_of(i * 16, 16), 16)
@@ -336,6 +380,20 @@
     store.start()
     stores.append(store)
 
+    loads[5].wait()
+    loads[6].wait()
+    for k in (0, 1):
+        here = pl.ds(k * HALF, HALF)
+        locals_sum = ztotal[pl.ds(4 * k, 4), :]
+        g = globv[:, here]
+        average = (32.0 * g - locals_sum) * (1.0 / 32.0)
+        momentum = 0.9 * momv[:, here] + average
+        nmomv[:, here] = momentum
+        nglobv[:, here] = g - 0.7 * (average + 0.9 * momentum)
+    for copy in (local(7, nglobv, nglob_o), local(8, nmomv, nmom_o)):
+        copy.start()
+        stores.append(copy)
+
     x_g.wait_recv()
     ggainv[:, pl.ds(pl.multiple_of(mine, 128), HALF)] = gsum[...]
     ggainv[:, pl.ds(pl.multiple_of(other, 128), HALF)] = gx_r[...]
@@ -383,28 +441,57 @@
             ag_copy(direction, j).wait_send()
             rs_copy(direction, j).wait_send()
         for hop in range(4 - direction):
-            z_send(direction, hop).wait_send()
             g_send(direction, hop).wait_send()
-    for copy in (x_c, x_n, x_dn, x_k, x_g, x_core, x_xhi):
+    for copy in (x_c, x_n, x_dn, x_k, x_g):
         copy.wait_send()
+
+    @pl.when(z < last)
+    def _():
+        z_up.wait_send()
+
+    @pl.when(z == last)
+    def _():
+        z_core.wait_send()
+        z_xhi.wait_send()
+
+    @pl.when(z > 0)
+    def _():
+        z_down.wait_send()
+
     for copy in stores:
         copy.wait()
 
 
+def hand_over(*refs):
+    sources, results, staged, sems = refs[:6], refs[6:12], refs[12:18], refs[18]
+    order = range(6)
+    ins = [pltpu.make_async_copy(sources[i], staged[i], sems.at[0, i]) for i in order]
+    outs = [pltpu.make_async_copy(staged[i], results[i], sems.at[1, i]) for i in order]
+    for copy in ins:
+        copy.start()
+    for i in order:
+        ins[i].wait()
+        outs[i].start()
+    for copy in outs:
+        copy.wait()
+
+
 def on_device(tokens, gain, key_weight, key_cotangent, local_fragment, global_fragment, outer_momentum):
     v, dma = pltpu.VMEM, pltpu.SemaphoreType.DMA
-    return pl.pallas_call(
+    hbm, anywhere = pl.BlockSpec(memory_space=pltpu.HBM), pl.BlockSpec(memory_space=pl.ANY)
+    shapes = (
+        jax.ShapeDtypeStruct((ROWS, KV), bf16),
+        jax.ShapeDtypeStruct((ROWS, D), bf16),
+        jax.ShapeDtypeStruct((1, SHARD, KV), bf16),
+        jax.ShapeDtypeStruct((1, D), f32),
+        jax.ShapeDtypeStruct((4, D), f32),
+        jax.ShapeDtypeStruct((4, D), f32),
+    )
+    outs = pl.pallas_call(
         kernel,
-        out_shape=(
-            jax.ShapeDtypeStruct((ROWS, KV), bf16),
-            jax.ShapeDtypeStruct((ROWS, D), bf16),
-            jax.ShapeDtypeStruct((1, SHARD, KV), bf16),
-            jax.ShapeDtypeStruct((1, D), f32),
-            jax.ShapeDtypeStruct((4, D), f32),
-            jax.ShapeDtypeStruct((4, D), f32),
-        ),
-        in_specs=[pl.BlockSpec(memory_space=pl.ANY)] * 7,
-        out_specs=[pl.BlockSpec(memory_space=pl.ANY)] * 6,
+        out_shape=shapes,
+        in_specs=[hbm] * 7,
+        out_specs=[anywhere] * 6,
         scratch_shapes=[
             v((ROWS, D), bf16),
             v((1, D), f32),
@@ -430,7 +517,8 @@
             v((4, D), f32),
             v((4, D), f32),
             v((4, D), f32),
-            v((RING, 8, HALF), f32),
+            v((8, HALF), f32),
+            v((8, HALF), f32),
             v((8, HALF), f32),
             v((8, HALF), f32),
             v((8, HALF), f32),
@@ -445,21 +533,27 @@
             dma((2, HOPS)),
             dma((5,)),
             dma((5,)),
+            dma((4,)),
+            dma((4,)),
             dma((2, 4)),
             dma((2, 4)),
-            dma((2, 4)),
-            dma((2, 4)),
-            dma((2,)),
-            dma((2,)),
+            pltpu.SemaphoreType.REGULAR,
             dma((13,)),
         ],
         compiler_params=pltpu.CompilerParams(
-            collective_id=0, has_side_effects=True, vmem_limit_bytes=52 * 2**20
+            collective_id=0, has_side_effects=True, vmem_limit_bytes=63 * 2**20
         ),
         cost_estimate=pl.CostEstimate(
             flops=6 * ROWS * D * KV, bytes_accessed=8 * 2**20, transcendentals=ROWS
         ),
     )(tokens, gain, key_weight, key_cotangent, local_fragment, global_fragment, outer_momentum)
+    return pl.pallas_call(
+        hand_over,
+        out_shape=shapes,
+        in_specs=[anywhere] * 6,
+        out_specs=[hbm] * 6,
+        scratch_shapes=[v(s.shape, s.dtype) for s in shapes] + [dma((2, 6))],
+    )(*outs)
 
 
 def solution(mesh):

time: 116 us -> 103 us (0.89); the launches traced: 116 us -> 101 us
  local copies, waits for them, and re-layouts: 10.2 us -> 0 us
  Pallas kernels: 105 us -> 100 us
    unnamed x16 -> x0, local copies, waits for them, and re-layouts: 10.2 us -> none
    pallas_call x1 -> x2, Pallas kernels: 105 us -> 100 us  [the longest x1 97.4 us: on_device(): pl.pallas_call(kernel, out_shape=shapes, in_specs=[hbm] * 7, out_specs=[a...]
where the time goes in v2:
time: 103 us; the launch traced here: 101 us
  Pallas kernels  100 us (97%)
    pallas_call x1, Pallas kernels, on_device(): pl.pallas_call(kernel, out_shape=shapes, in_specs=[hbm] * 7, out_specs=[a...  97.4 us
    pallas_call x1, Pallas kernels, on_device(): pl.pallas_call(hand_over, out_shape=shapes, in_specs=[anywhere] * 6, out_...  2.93 us

profile of v2, /device:TPU:6, one launch (start us, length us, event | category | flops | bytes accessed | tf_op | source)
XLA Modules:
  0.0 101.0 jit_solution(4754095340534691019)
XLA Ops:
  0.6 97.4 %shard_map.118 = (bf16[160,1024]{1,0:T(8,128)(2,1)}, bf16[160,4608]{1,0:T(8,128)(2,1)}, bf16[1,288,1024]{2,1,0:T(8,128)(2,1)}, f32[1,4608]{1,0:T(1,128)}, f32[4,4608]{1,0:T(4,128)}, /*index=5*/f32[4,4608]{1,0:T(4,128)}) custom-call(bf16[160,4608]{1,0:T(8,128)(2,1)} %tok.1, f32[1,4608]{1,0:T(1,128)} %gain.1, bf16[1,288,1024]{2,1,0:T(8,128)(2,1)} %w.1, ...), custom_call_target="tpu_custom_call" | custom-call | flops 4529848320 | bytes 8388608 | tf_op jit(solution)/shard_map/pallas_call | solution.py:490
  98.1 2.9 %shard_map.119 = (bf16[160,1024]{1,0:T(8,128)(2,1)}, bf16[160,4608]{1,0:T(8,128)(2,1)}, bf16[1,288,1024]{2,1,0:T(8,128)(2,1)}, f32[1,4608]{1,0:T(1,128)}, f32[4,4608]{1,0:T(4,128)}, /*index=5*/f32[4,4608]{1,0:T(4,128)}) custom-call(bf16[160,1024]{1,0:T(8,128)(2,1)} %get-tuple-element.12.refs_0_, bf16[160,4608]{1,0:T(8,128)(2,1)} %get-tuple-element.13.refs_1_, ...), custom_call_target="tpu_custom_call" | custom-call | tf_op jit(solution)/shard_map/pallas_call | solution.py:550

commit v3 on v2

--- a/solution.py
+++ b/solution.py
@@ -19,15 +19,17 @@
 SHARD = 288
 PIECE = SHARD // 2
 HOPS = 7
+CUTS = 3
+CUT = PIECE // CUTS
 
 
 def kernel(
     tok, gain, w, cot, frag, glob, mom,
     keys_o, gtok_o, gw_o, ggain_o, nglob_o, nmom_o,
     tokv, gainv, n2, nsend, c2, wall, part, rs_s, rs_r, dn_own, dn_s, dn_r, k_own, k_s, k_r,
-    rstdv, gtokv, keysv, gwv, fragv, globv, momv, nglobv, nmomv,
-    zacc, zin_r, core_r, csum, xhi_r, ztotal, gring, gsum, gx_r, ggainv,
-    ag_ss, ag_rs, rs_ss, rs_rs, x_ss, x_rs, z_ss, z_rs, g_ss, g_rs, above_in, loc,
+    rstdv, fragv, globv, momv,
+    zacc, zin_r, core_r, csum, xhi_r, ztotal, gring, gsum, gx_r,
+    ag_ss, ag_rs, rs_ss, rs_rs, x_ss, x_rs, z_ss, z_rs, g_ss, g_rs, above_in, partner_in, core_in, xhi_in, loc,
 ):
     me = lax.axis_index("fsdp")
     rep = lax.axis_index("replica")
@@ -66,32 +68,44 @@
         local(5, glob, globv),
         local(6, mom, momv),
     ]
-    for copy in loads:
-        copy.start()
 
     barrier = pltpu.get_barrier_semaphore()
 
     def greet(peer):
         pl.semaphore_signal(barrier, inc=1, device_id=peer, device_id_type=MESH)
 
-    for peer in ring + (partner,):
+    for peer in ring:
         greet(peer)
+
+    at_top = z == last
+    pairs = (
+        (True, x == 0, partner, partner_in),
+        (at_top, core == 1, core_dev, core_in),
+        (at_top, xhi == 0, xhi_dev, xhi_in),
+    )
 
     @pl.when(z < last)
     def _():
         greet(above)
 
-    @pl.when(z == last)
-    def _():
-        greet(core_dev)
-        greet(xhi_dev)
-
-    greeted = 3 + jnp.where(z > 0, 1, 0) + jnp.where(z == last, 2, 0)
+    greeted = 2 + jnp.where(z > 0, 1, 0)
+    for member, earlier, peer, _ in pairs:
+        pl.when(earlier & member)(functools.partial(greet, peer))
+        greeted = greeted + jnp.where((~earlier) & member, 1, 0)
+    for copy in loads:
+        copy.start()
     pl.semaphore_wait(barrier, greeted)
 
-    @pl.when(z > 0)
-    def _():
-        pl.semaphore_signal(above_in, inc=1, device_id=below, device_id_type=MESH)
+    def tell(peer, sem):
+        pl.semaphore_signal(sem, inc=1, device_id=peer, device_id_type=MESH)
+
+    pl.when(z > 0)(functools.partial(tell, below, above_in))
+    for member, earlier, peer, sem in pairs:
+        pl.when((~earlier) & member)(functools.partial(tell, peer, sem))
+
+    def know(pair):
+        member, earlier, _, sem = pair
+        pl.when(earlier & member)(lambda: pl.semaphore_wait(sem, 1))
 
     def wpiece(direction, j, extra):
         away = j // 2 + extra
@@ -124,6 +138,7 @@
     x_k = remote(k_s, k_r, x_ss.at[3], x_rs.at[3], partner)
     x_g = remote(gsum, gx_r, x_ss.at[4], x_rs.at[4], partner)
     loads[3].wait()
+    know(pairs[0])
     x_c.start()
 
     def small_ring(buf, at, ss, rs, devs):
@@ -166,6 +181,9 @@
                 z_up.start()
 
         if high == last:
+
+            know(pairs[1])
+            know(pairs[2])
 
             @pl.when(z == last)
             def _():
@@ -251,39 +269,36 @@
     ag_arrive(4)
     z_turn_x()
 
-    def part_rows(direction, away, half, i):
+    def part_rows(direction, away, half, cut):
         shard = (y + away) % RING if direction == 0 else (y + RING - away) % RING
-        return pl.ds(pl.multiple_of(shard * SHARD + half * PIECE + i * 16, 16), 16)
-
-    def rs_copy(direction, j):
+        return pl.ds(pl.multiple_of(shard * SHARD + half * PIECE + cut * CUT, 16), CUT)
+
+    def rs_copy(direction, j, cut):
+        rows = pl.ds(cut * CUT, CUT)
         return remote(
-            rs_s.at[direction, j], rs_r.at[direction, j],
-            rs_ss.at[direction, j], rs_rs.at[direction, j], ring[direction],
+            rs_s.at[direction, j, rows], rs_r.at[direction, j, rows],
+            rs_ss.at[direction, j, cut], rs_rs.at[direction, j, cut], ring[direction],
         )
 
-    def rs_send(direction, j):
+    def rs_send(direction, j, cut):
         half, away = (j % 2) ^ direction, 4 - (j + 1) // 2
-
-        def block(i, _):
-            rows = pl.ds(pl.multiple_of(i * 16, 16), 16)
-            v = part[part_rows(direction, away, half, i), :]
-            if j >= 2:
-                v = v + rs_r[direction, j - 2, rows, :].astype(f32)
-            rs_s[direction, j, rows, :] = v.astype(bf16)
-            return 0
-
-        lax.fori_loop(0, PIECE // 16, block, 0)
-        rs_copy(direction, j).start()
+        rows = pl.ds(cut * CUT, CUT)
+        v = part[part_rows(direction, away, half, cut), :]
+        if j >= 2:
+            v = v + rs_r[direction, j - 2, rows, :].astype(f32)
+        rs_s[direction, j, rows, :] = v.astype(bf16)
+        rs_copy(direction, j, cut).start()
 
     def rs_arrive(j):
-        for direction in (0, 1):
-            rs_copy(direction, j).wait_recv()
-            if j + 2 < HOPS:
-                rs_send(direction, j + 2)
+        for cut in range(CUTS):
+            for direction in (0, 1):
+                rs_copy(direction, j, cut).wait_recv()
+                rs_send(direction, j + 2, cut)
 
     for j in (0, 1):
-        for direction in (0, 1):
-            rs_send(direction, j)
+        for cut in range(CUTS):
+            for direction in (0, 1):
+                rs_send(direction, j, cut)
 
     ag_arrive(5)
     z_fall(6)
@@ -332,8 +347,6 @@
     z_fall(1)
     g_arrive(3)
 
-    stores = []
-
     total = gring[0]
     for k in range(1, RING):
         total = total + gring[k]
@@ -344,13 +357,10 @@
 
     def keys_block(i, _):
         rows = pl.ds(pl.multiple_of(i * 16, 16), 16)
-        keysv[rows, :] = (k_own[rows, :] + k_r[rows, :].astype(f32)).astype(bf16)
+        keys_o[rows, :] = (k_own[rows, :] + k_r[rows, :].astype(f32)).astype(bf16)
         return 0
 
     lax.fori_loop(0, ROWS // 16, keys_block, 0)
-    store = local(9, keysv, keys_o)
-    store.start()
-    stores.append(store)
 
     x_dn.wait_recv()
     rs_arrive(4)
@@ -372,13 +382,10 @@
             for at in range(0, HALF, step):
                 unit = tokv[rows, cols(base, at)].astype(f32) * rstd
                 scaled = grad[rows, pl.ds(at, step)].astype(f32) * (1.0 + gainv[:, cols(base, at)])
-                gtokv[rows, cols(base, at)] = (rstd * (scaled - unit * mean)).astype(bf16)
+                gtok_o[rows, cols(base, at)] = (rstd * (scaled - unit * mean)).astype(bf16)
         return 0
 
     lax.fori_loop(0, ROWS // 16, gtok_block, 0)
-    store = local(10, gtokv, gtok_o)
-    store.start()
-    stores.append(store)
 
     loads[5].wait()
     loads[6].wait()
@@ -388,58 +395,30 @@
         g = globv[:, here]
         average = (32.0 * g - locals_sum) * (1.0 / 32.0)
         momentum = 0.9 * momv[:, here] + average
-        nmomv[:, here] = momentum
-        nglobv[:, here] = g - 0.7 * (average + 0.9 * momentum)
-    for copy in (local(7, nglobv, nglob_o), local(8, nmomv, nmom_o)):
-        copy.start()
-        stores.append(copy)
+        nmom_o[:, here] = momentum
+        nglob_o[:, here] = g - 0.7 * (average + 0.9 * momentum)
 
     x_g.wait_recv()
-    ggainv[:, pl.ds(pl.multiple_of(mine, 128), HALF)] = gsum[...]
-    ggainv[:, pl.ds(pl.multiple_of(other, 128), HALF)] = gx_r[...]
-    store = local(11, ggainv, ggain_o)
-    store.start()
-    stores.append(store)
-
-    rs_arrive(5)
-
-    def early_block(direction):
-        half = 1 - direction
-
-        def block(i, _):
-            rows = part_rows(0, 0, half, i)
-            arrived = rs_r[direction, 5, pl.ds(pl.multiple_of(i * 16, 16), 16), :]
-            part[rows, :] = part[rows, :] + arrived.astype(f32)
-            return 0
-
-        return block
-
-    for direction in (0, 1):
-        lax.fori_loop(0, PIECE // 16, early_block(direction), 0)
-    rs_arrive(6)
-
-    def last_block(direction):
-        half = direction
-
-        def block(i, _):
-            arrived = rs_r[direction, 6, pl.ds(pl.multiple_of(i * 16, 16), 16), :]
-            to = pl.ds(pl.multiple_of(half * PIECE + i * 16, 16), 16)
-            v = part[part_rows(0, 0, half, i), :] + arrived.astype(f32)
-            gwv[to, :] = v.astype(bf16)
-            return 0
-
-        return block
-
-    for direction in (0, 1):
-        lax.fori_loop(0, PIECE // 16, last_block(direction), 0)
-    store = local(12, gwv, gw_o.at[0])
-    store.start()
-    stores.append(store)
+    ggain_o[:, pl.ds(pl.multiple_of(mine, 128), HALF)] = gsum[...]
+    ggain_o[:, pl.ds(pl.multiple_of(other, 128), HALF)] = gx_r[...]
+
+    for cut in range(CUTS):
+        for direction in (0, 1):
+            rs_copy(direction, 5, cut).wait_recv()
+            rows = part_rows(0, 0, 1 - direction, cut)
+            part[rows, :] = part[rows, :] + rs_r[direction, 5, pl.ds(cut * CUT, CUT), :].astype(f32)
+    for cut in range(CUTS):
+        for direction in (0, 1):
+            rs_copy(direction, 6, cut).wait_recv()
+            v = part[part_rows(0, 0, direction, cut), :]
+            v = v + rs_r[direction, 6, pl.ds(cut * CUT, CUT), :].astype(f32)
+            gw_o[0, pl.ds(direction * PIECE + cut * CUT, CUT), :] = v.astype(bf16)
 
     for direction in (0, 1):
         for j in range(HOPS):
             ag_copy(direction, j).wait_send()
-            rs_copy(direction, j).wait_send()
+            for cut in range(CUTS):
+                rs_copy(direction, j, cut).wait_send()
         for hop in range(4 - direction):
             g_send(direction, hop).wait_send()
     for copy in (x_c, x_n, x_dn, x_k, x_g):
@@ -458,21 +437,16 @@
     def _():
         z_down.wait_send()
 
-    for copy in stores:
-        copy.wait()
-
 
 def hand_over(*refs):
-    sources, results, staged, sems = refs[:6], refs[6:12], refs[12:18], refs[18]
-    order = range(6)
-    ins = [pltpu.make_async_copy(sources[i], staged[i], sems.at[0, i]) for i in order]
-    outs = [pltpu.make_async_copy(staged[i], results[i], sems.at[1, i]) for i in order]
-    for copy in ins:
+    sources, results, sems = refs[:6], refs[6:12], refs[12]
+    copies = [
+        pltpu.make_async_copy(src, dst, sems.at[i])
+        for i, (src, dst) in enumerate(zip(sources, results))
+    ]
+    for copy in copies:
         copy.start()
-    for i in order:
-        ins[i].wait()
-        outs[i].start()
-    for copy in outs:
+    for copy in copies:
         copy.wait()
 
 
@@ -487,11 +461,13 @@
         jax.ShapeDtypeStruct((4, D), f32),
         jax.ShapeDtypeStruct((4, D), f32),
     )
+    args = (tokens, gain, key_weight, key_cotangent, local_fragment, global_fragment, outer_momentum)
+    args = [pltpu.with_memory_space_constraint(a, pltpu.HBM) for a in args]
     outs = pl.pallas_call(
         kernel,
-        out_shape=shapes,
+        out_shape=[v(s.shape, s.dtype) for s in shapes],
         in_specs=[hbm] * 7,
-        out_specs=[anywhere] * 6,
+        out_specs=[pl.BlockSpec(memory_space=pltpu.VMEM)] * 6,
         scratch_shapes=[
             v((ROWS, D), bf16),
             v((1, D), f32),
@@ -509,12 +485,7 @@
             v((ROWS, KV), bf16),
             v((ROWS, KV), bf16),
             v((ROWS, 128), f32),
-            v((ROWS, D), bf16),
-            v((ROWS, KV), bf16),
-            v((SHARD, KV), bf16),
             v((4, D), bf16),
-            v((4, D), f32),
-            v((4, D), f32),
             v((4, D), f32),
             v((4, D), f32),
             v((8, HALF), f32),
@@ -526,11 +497,10 @@
             v((RING, 1, HALF), f32),
             v((1, HALF), f32),
             v((1, HALF), f32),
-            v((1, D), f32),
             dma((2, HOPS)),
             dma((2, HOPS)),
-            dma((2, HOPS)),
-            dma((2, HOPS)),
+            dma((2, HOPS, CUTS)),
+            dma((2, HOPS, CUTS)),
             dma((5,)),
             dma((5,)),
             dma((4,)),
@@ -538,22 +508,26 @@
             dma((2, 4)),
             dma((2, 4)),
             pltpu.SemaphoreType.REGULAR,
-            dma((13,)),
+            pltpu.SemaphoreType.REGULAR,
+            pltpu.SemaphoreType.REGULAR,
+            pltpu.SemaphoreType.REGULAR,
+            dma((7,)),
         ],
         compiler_params=pltpu.CompilerParams(
-            collective_id=0, has_side_effects=True, vmem_limit_bytes=63 * 2**20
+            collective_id=0, has_side_effects=True, vmem_limit_bytes=48 * 2**20
         ),
         cost_estimate=pl.CostEstimate(
             flops=6 * ROWS * D * KV, bytes_accessed=8 * 2**20, transcendentals=ROWS
         ),
-    )(tokens, gain, key_weight, key_cotangent, local_fragment, global_fragment, outer_momentum)
+    )(*args)
     return pl.pallas_call(
         hand_over,
         out_shape=shapes,
         in_specs=[anywhere] * 6,
         out_specs=[hbm] * 6,
-        scratch_shapes=[v(s.shape, s.dtype) for s in shapes] + [dma((2, 6))],
-    )(*outs)
+        scratch_shapes=[dma((6,))],
+        compiler_params=pltpu.CompilerParams(vmem_limit_bytes=2**20),
+    )(*[pltpu.with_memory_space_constraint(a, pltpu.VMEM) for a in outs])
 
 
 def solution(mesh):

time: 103 us -> 99.4 us (0.965); the launches traced: 101 us -> 99.1 us
  Pallas kernels: 100 us -> 98.5 us
    pallas_call x1, Pallas kernels: 2.93 us -> 1.51 us  [on_device(): pl.pallas_call(hand_over, out_shape=shapes, in_specs=[anywhere] * 6, out_...]
where the time goes in v3:
time: 99.4 us; the launch traced here: 99.1 us
  Pallas kernels  98.5 us (99%)
    pallas_call x1, Pallas kernels, on_device(): pl.pallas_call(kernel, out_shape=[v(s.shape, s.dtype) for s in shapes], i...  97 us

profile of v3, /device:TPU:6, one launch (start us, length us, event | category | flops | bytes accessed | tf_op | source)
XLA Modules:
  0.0 99.1 jit_solution(9833668755695467838)
XLA Ops:
  0.6 97.0 %shard_map.118 = (bf16[160,1024]{1,0:T(8,128)(2,1)S(1)}, bf16[160,4608]{1,0:T(8,128)(2,1)S(1)}, bf16[1,288,1024]{2,1,0:T(8,128)(2,1)S(1)}, f32[1,4608]{1,0:T(1,1...) custom-call(bf16[160,4608]{1,0:T(8,128)(2,1)} %tok.1, f32[1,4608]{1,0:T(1,128)} %gain.1, bf16[1,288,1024]{2,1,0:T(8,128)(2,1)} %w.1, ...), custom_call_target="tpu_custom_call" | custom-call | flops 4529848320 | bytes 8388608 | tf_op jit(solution)/shard_map/pallas_call | solution.py:466
  97.6 1.5 %shard_map.119 = (bf16[160,1024]{1,0:T(8,128)(2,1)}, bf16[160,4608]{1,0:T(8,128)(2,1)}, bf16[1,288,1024]{2,1,0:T(8,128)(2,1)}, f32[1,4608]{1,0:T(1,128)}, f32[4,4608]{1,0:T(4,128)}, /*index=5*/f32[4,4608]{1,0:T(4,128)}) custom-call(bf16[160,1024]{1,0:T(8,128)(2,1)S(1)} %get-tuple-element.12.refs_0_, bf16[160,4608]{1,0:T(8,128)(2,1)S(1)} %get-tuple-element.13.refs_1_, ...), custom_call_target="tpu_custom_call" | custom-call | tf_op jit(solution)/shard_map/pallas_call | solution.py:523

commit v4 on v3

--- a/solution.py
+++ b/solution.py
@@ -19,7 +19,7 @@
 SHARD = 288
 PIECE = SHARD // 2
 HOPS = 7
-CUTS = 3
+CUTS = 1
 CUT = PIECE // CUTS
 
 
@@ -28,8 +28,8 @@
     keys_o, gtok_o, gw_o, ggain_o, nglob_o, nmom_o,
     tokv, gainv, n2, nsend, c2, wall, part, rs_s, rs_r, dn_own, dn_s, dn_r, k_own, k_s, k_r,
     rstdv, fragv, globv, momv,
-    zacc, zin_r, core_r, csum, xhi_r, ztotal, gring, gsum, gx_r,
-    ag_ss, ag_rs, rs_ss, rs_rs, x_ss, x_rs, z_ss, z_rs, g_ss, g_rs, above_in, partner_in, core_in, xhi_in, loc,
+    nt, cn, pk_s, pk_r, zacc, zin_r, core_r, csum, xhi_r, ztotal, gring, gsum, gx_r,
+    ag_ss, ag_rs, rs_ss, rs_rs, f_ss, f_rs, x_ss, x_rs, z_ss, z_rs, g_ss, g_rs, above_in, partner_in, core_in, xhi_in, loc,
 ):
     me = lax.axis_index("fsdp")
     rep = lax.axis_index("replica")
@@ -140,6 +140,29 @@
     loads[3].wait()
     know(pairs[0])
     x_c.start()
+
+    own, theirs = pl.ds(0, ROWS), pl.ds(ROWS, ROWS)
+
+    def fc_copy(direction):
+        return remote(
+            c2.at[own], cn.at[direction, own],
+            f_ss.at[0, direction], f_rs.at[0, direction], ring[direction],
+        )
+
+    def fx_copy(direction):
+        return remote(
+            cn.at[direction, own], cn.at[direction, theirs],
+            f_ss.at[1, direction], f_rs.at[1, direction], partner,
+        )
+
+    def fn_copy(direction):
+        return remote(
+            pk_s.at[direction], pk_r.at[direction],
+            f_ss.at[2, direction], f_rs.at[2, direction], ring[direction],
+        )
+
+    for direction in (0, 1):
+        fc_copy(direction).start()
 
     def small_ring(buf, at, ss, rs, devs):
         def slot(direction, hop):
@@ -248,10 +271,12 @@
     z_rise(1, 2)
     ag_arrive(1)
     z_rise(3, 4)
-    ag_arrive(2)
+    for direction in (0, 1):
+        fc_copy(direction).wait_recv()
+        fx_copy(direction).start()
     z_rise(5, 6)
     z_rise(7, 7)
-    ag_arrive(3)
+    ag_arrive(2)
     z_turn_core()
 
     x_c.wait_recv()
@@ -259,15 +284,12 @@
 
     def part_block(i, _):
         at = pl.multiple_of(i * 256, 256)
-        part[pl.ds(at, 256), :] = lax.dot_general(
-            n2[:, pl.ds(at, 256)], c2[...], (((0,), (0,)), ((), ())), preferred_element_type=f32
-        )
+        turned = n2[:, pl.ds(at, 256)].T
+        nt[pl.ds(at, 256), :] = turned
+        part[pl.ds(at, 256), :] = jnp.dot(turned, c2[...], preferred_element_type=f32)
         return 0
 
     lax.fori_loop(0, HALF // 256, part_block, 0)
-
-    ag_arrive(4)
-    z_turn_x()
 
     def part_rows(direction, away, half, cut):
         shard = (y + away) % RING if direction == 0 else (y + RING - away) % RING
@@ -284,26 +306,50 @@
         half, away = (j % 2) ^ direction, 4 - (j + 1) // 2
         rows = pl.ds(cut * CUT, CUT)
         v = part[part_rows(direction, away, half, cut), :]
-        if j >= 2:
+        if j >= 4:
             v = v + rs_r[direction, j - 2, rows, :].astype(f32)
+        else:
+            factor = (pk_r[direction, rows, pl.ds((j - 2) * 256, 256)], pk_r[direction, rows, pl.ds(512, 128)])
+            zero = jnp.zeros((64, KV), bf16)
+            rest = cn[direction, pl.ds(256, 64), :]
+            rest = jnp.concatenate([rest, zero] if j == 2 else [zero, rest], axis=0)
+            v = v + jnp.dot(factor[0], cn[direction, pl.ds(0, 256), :], preferred_element_type=f32)
+            v = v + jnp.dot(factor[1], rest, preferred_element_type=f32)
         rs_s[direction, j, rows, :] = v.astype(bf16)
         rs_copy(direction, j, cut).start()
 
     def rs_arrive(j):
-        for cut in range(CUTS):
-            for direction in (0, 1):
-                rs_copy(direction, j, cut).wait_recv()
-                rs_send(direction, j + 2, cut)
-
-    for j in (0, 1):
-        for cut in range(CUTS):
-            for direction in (0, 1):
-                rs_send(direction, j, cut)
+        for direction in (0, 1):
+            rs_copy(direction, j, 0).wait_recv()
+        g_arrive(j - 2)
+        for direction in (0, 1):
+            rs_send(direction, j + 2, 0)
+
+    def pack(direction):
+        a, b = (nt[part_rows(direction, 4 - j, (j % 2) ^ direction, 0), :] for j in (0, 1))
+        pk_s[direction, :, :] = jnp.concatenate(
+            [a[:, :256], b[:, :256], a[:, 256:], b[:, 256:]], axis=1
+        )
+        fn_copy(direction).start()
+
+    for direction in (0, 1):
+        pack(direction)
+
+    ag_arrive(3)
+    z_turn_x()
+
+    ag_arrive(4)
+    z_fall(6)
+
+    for direction in (0, 1):
+        fn_copy(direction).wait_recv()
+        fx_copy(direction).wait_recv()
+        rs_send(direction, 2, 0)
 
     ag_arrive(5)
-    z_fall(6)
+    z_fall(5)
     ag_arrive(6)
-    z_fall(5)
+    z_fall(4)
     loads[4].wait()
 
     def dn_block(i, _):
@@ -322,6 +368,8 @@
     x_dn.start()
     g_send(0, 0).start()
     g_send(1, 0).start()
+    rs_send(0, 3, 0)
+    rs_send(1, 3, 0)
 
     def key_block(i, _):
         at = pl.multiple_of(i * 256, 256)
@@ -333,38 +381,14 @@
     lax.fori_loop(0, KV // 256, key_block, 0)
     x_k.start()
 
-    rs_arrive(0)
-    z_fall(4)
-    g_arrive(0)
-
-    rs_arrive(1)
+    rs_arrive(2)
     z_fall(3)
-    g_arrive(1)
-    rs_arrive(2)
+    rs_arrive(3)
     z_fall(2)
-    g_arrive(2)
-    rs_arrive(3)
+    rs_arrive(4)
     z_fall(1)
-    g_arrive(3)
-
-    total = gring[0]
-    for k in range(1, RING):
-        total = total + gring[k]
-    gsum[...] = total / (1.0 + gainv[:, pl.ds(pl.multiple_of(mine, 128), HALF)])
-    x_g.start()
-
-    x_k.wait_recv()
-
-    def keys_block(i, _):
-        rows = pl.ds(pl.multiple_of(i * 16, 16), 16)
-        keys_o[rows, :] = (k_own[rows, :] + k_r[rows, :].astype(f32)).astype(bf16)
-        return 0
-
-    lax.fori_loop(0, ROWS // 16, keys_block, 0)
 
     x_dn.wait_recv()
-    rs_arrive(4)
-    z_fall(0)
 
     def gtok_block(i, _):
         rows = pl.ds(pl.multiple_of(i * 16, 16), 16)
@@ -387,6 +411,20 @@
 
     lax.fori_loop(0, ROWS // 16, gtok_block, 0)
 
+    for cut in range(CUTS):
+        for direction in (0, 1):
+            rs_copy(direction, 5, cut).wait_recv()
+            rows = part_rows(0, 0, 1 - direction, cut)
+            part[rows, :] = part[rows, :] + rs_r[direction, 5, pl.ds(cut * CUT, CUT), :].astype(f32)
+    z_fall(0)
+    g_arrive(3)
+
+    total = gring[0]
+    for k in range(1, RING):
+        total = total + gring[k]
+    gsum[...] = total / (1.0 + gainv[:, pl.ds(pl.multiple_of(mine, 128), HALF)])
+    x_g.start()
+
     loads[5].wait()
     loads[6].wait()
     for k in (0, 1):
@@ -398,15 +436,15 @@
         nmom_o[:, here] = momentum
         nglob_o[:, here] = g - 0.7 * (average + 0.9 * momentum)
 
-    x_g.wait_recv()
-    ggain_o[:, pl.ds(pl.multiple_of(mine, 128), HALF)] = gsum[...]
-    ggain_o[:, pl.ds(pl.multiple_of(other, 128), HALF)] = gx_r[...]
-
-    for cut in range(CUTS):
-        for direction in (0, 1):
-            rs_copy(direction, 5, cut).wait_recv()
-            rows = part_rows(0, 0, 1 - direction, cut)
-            part[rows, :] = part[rows, :] + rs_r[direction, 5, pl.ds(cut * CUT, CUT), :].astype(f32)
+    x_k.wait_recv()
+
+    def keys_block(i, _):
+        rows = pl.ds(pl.multiple_of(i * 16, 16), 16)
+        keys_o[rows, :] = (k_own[rows, :] + k_r[rows, :].astype(f32)).astype(bf16)
+        return 0
+
+    lax.fori_loop(0, ROWS // 16, keys_block, 0)
+
     for cut in range(CUTS):
         for direction in (0, 1):
             rs_copy(direction, 6, cut).wait_recv()
@@ -414,11 +452,18 @@
             v = v + rs_r[direction, 6, pl.ds(cut * CUT, CUT), :].astype(f32)
             gw_o[0, pl.ds(direction * PIECE + cut * CUT, CUT), :] = v.astype(bf16)
 
+    x_g.wait_recv()
+    ggain_o[:, pl.ds(pl.multiple_of(mine, 128), HALF)] = gsum[...]
+    ggain_o[:, pl.ds(pl.multiple_of(other, 128), HALF)] = gx_r[...]
+
     for direction in (0, 1):
         for j in range(HOPS):
             ag_copy(direction, j).wait_send()
-            for cut in range(CUTS):
-                rs_copy(direction, j, cut).wait_send()
+            if j >= 2:
+                for cut in range(CUTS):
+                    rs_copy(direction, j, cut).wait_send()
+        for copy in (fc_copy, fx_copy, fn_copy):
+            copy(direction).wait_send()
         for hop in range(4 - direction):
             g_send(direction, hop).wait_send()
     for copy in (x_c, x_n, x_dn, x_k, x_g):
@@ -488,6 +533,10 @@
             v((4, D), bf16),
             v((4, D), f32),
             v((4, D), f32),
+            v((HALF, 2 * ROWS), bf16),
+            v((2, 2 * ROWS, KV), bf16),
+            v((2, PIECE, 4 * ROWS), bf16),
+            v((2, PIECE, 4 * ROWS), bf16),
             v((8, HALF), f32),
             v((8, HALF), f32),
             v((8, HALF), f32),
@@ -501,6 +550,8 @@
             dma((2, HOPS)),
             dma((2, HOPS, CUTS)),
             dma((2, HOPS, CUTS)),
+            dma((3, 2)),
+            dma((3, 2)),
             dma((5,)),
             dma((5,)),
             dma((4,)),

time: 99.4 us -> 97.4 us (0.980)
  Pallas kernels: 98.5 us -> 96.5 us
    pallas_call x1, Pallas kernels: 97 us -> 95 us  [on_device(): pl.pallas_call(kernel, out_shape=[v(s.shape, s.dtype) for s in shapes], i...]
where the time goes in v4:
time: 97.4 us; the launch traced here: 97.1 us
  Pallas kernels  96.5 us (99%)
    pallas_call x1, Pallas kernels, on_device(): pl.pallas_call(kernel, out_shape=[v(s.shape, s.dtype) for s in shapes], i...  95 us

profile of v4, /device:TPU:6, one launch (start us, length us, event | category | flops | bytes accessed | tf_op | source)
XLA Modules:
  0.0 97.1 jit_solution(9993003008411688505)
XLA Ops:
  0.6 95.0 %shard_map.118 = (bf16[160,1024]{1,0:T(8,128)(2,1)S(1)}, bf16[160,4608]{1,0:T(8,128)(2,1)S(1)}, bf16[1,288,1024]{2,1,0:T(8,128)(2,1)S(1)}, f32[1,4608]{1,0:T(1,1...) custom-call(bf16[160,4608]{1,0:T(8,128)(2,1)} %tok.1, f32[1,4608]{1,0:T(1,128)} %gain.1, bf16[1,288,1024]{2,1,0:T(8,128)(2,1)} %w.1, ...), custom_call_target="tpu_custom_call" | custom-call | flops 4529848320 | bytes 8388608 | tf_op jit(solution)/shard_map/pallas_call | solution.py:511
  95.6 1.5 %shard_map.119 = (bf16[160,1024]{1,0:T(8,128)(2,1)}, bf16[160,4608]{1,0:T(8,128)(2,1)}, bf16[1,288,1024]{2,1,0:T(8,128)(2,1)}, f32[1,4608]{1,0:T(1,128)}, f32[4,4608]{1,0:T(4,128)}, /*index=5*/f32[4,4608]{1,0:T(4,128)}) custom-call(bf16[160,1024]{1,0:T(8,128)(2,1)S(1)} %get-tuple-element.12.refs_0_, bf16[160,4608]{1,0:T(8,128)(2,1)S(1)} %get-tuple-element.13.refs_1_, ...), custom_call_target="tpu_custom_call" | custom-call | tf_op jit(solution)/shard_map/pallas_call | solution.py:574

commit v5 on v4

--- a/solution.py
+++ b/solution.py
@@ -117,15 +117,16 @@
         there = wpiece(direction, j, 0)
         half = (j % 2) ^ direction
         src = w.at[0, pl.ds(half * PIECE, PIECE)] if j < 2 else there
-        return remote(src, there, ag_ss.at[direction, j], ag_rs.at[direction, j], ring[direction])
+        return remote(src, there, ag_ss.at[direction, j % 2], ag_rs.at[direction, j], ring[direction])
 
     def ag_arrive(j):
         for direction in (0, 1):
             here = wpiece(direction, j, 1)
             remote(
-                here, here, ag_ss.at[direction, j], ag_rs.at[direction, j], ring[direction]
+                here, here, ag_ss.at[direction, j % 2], ag_rs.at[direction, j], ring[direction]
             ).wait_recv()
             if j + 2 < HOPS:
+                ag_copy(direction, j).wait_send()
                 ag_copy(direction, j + 2).start()
 
     for j in (0, 1):
@@ -171,7 +172,7 @@
         def send(direction, hop):
             return remote(
                 slot(direction, hop), slot(direction, hop),
-                ss.at[direction, hop], rs.at[direction, hop], devs[direction],
+                ss.at[direction], rs.at[direction, hop], devs[direction],
             )
 
         def arrive(hop):
@@ -179,9 +180,10 @@
                 if hop < 4 - direction:
                     here = slot(direction, hop + 1)
                     remote(
-                        here, here, ss.at[direction, hop], rs.at[direction, hop], devs[direction]
+                        here, here, ss.at[direction], rs.at[direction, hop], devs[direction]
                     ).wait_recv()
                     if hop + 1 < 4 - direction:
+                        send(direction, hop).wait_send()
                         send(direction, hop + 1).start()
 
         return send, arrive
@@ -299,7 +301,7 @@
         rows = pl.ds(cut * CUT, CUT)
         return remote(
             rs_s.at[direction, j, rows], rs_r.at[direction, j, rows],
-            rs_ss.at[direction, j, cut], rs_rs.at[direction, j, cut], ring[direction],
+            rs_ss.at[direction, j % 2, cut], rs_rs.at[direction, j - 2, cut], ring[direction],
         )
 
     def rs_send(direction, j, cut):
@@ -316,6 +318,8 @@
             v = v + jnp.dot(factor[0], cn[direction, pl.ds(0, 256), :], preferred_element_type=f32)
             v = v + jnp.dot(factor[1], rest, preferred_element_type=f32)
         rs_s[direction, j, rows, :] = v.astype(bf16)
+        if j >= 4:
+            rs_copy(direction, j - 2, cut).wait_send()
         rs_copy(direction, j, cut).start()
 
     def rs_arrive(j):
@@ -457,15 +461,13 @@
     ggain_o[:, pl.ds(pl.multiple_of(other, 128), HALF)] = gx_r[...]
 
     for direction in (0, 1):
-        for j in range(HOPS):
+        for j in (HOPS - 2, HOPS - 1):
             ag_copy(direction, j).wait_send()
-            if j >= 2:
-                for cut in range(CUTS):
-                    rs_copy(direction, j, cut).wait_send()
+            for cut in range(CUTS):
+                rs_copy(direction, j, cut).wait_send()
         for copy in (fc_copy, fx_copy, fn_copy):
             copy(direction).wait_send()
-        for hop in range(4 - direction):
-            g_send(direction, hop).wait_send()
+        g_send(direction, 3 - direction).wait_send()
     for copy in (x_c, x_n, x_dn, x_k, x_g):
         copy.wait_send()
 
@@ -546,17 +548,17 @@
             v((RING, 1, HALF), f32),
             v((1, HALF), f32),
             v((1, HALF), f32),
+            dma((2, 2)),
             dma((2, HOPS)),
-            dma((2, HOPS)),
-            dma((2, HOPS, CUTS)),
-            dma((2, HOPS, CUTS)),
+            dma((2, 2, CUTS)),
+            dma((2, HOPS - 2, CUTS)),
             dma((3, 2)),
             dma((3, 2)),
             dma((5,)),
             dma((5,)),
             dma((4,)),
             dma((4,)),
-            dma((2, 4)),
+            dma((2,)),
             dma((2, 4)),
             pltpu.SemaphoreType.REGULAR,
             pltpu.SemaphoreType.REGULAR,

time: 97.4 us -> 97.1 us (level)
  no operation moved by 1% of the time
where the time goes in v5:
time: 97.1 us; the launch traced here: 96.8 us
  Pallas kernels  96.2 us (99%)
    pallas_call x1, Pallas kernels, on_device(): pl.pallas_call(kernel, out_shape=[v(s.shape, s.dtype) for s in shapes], i...  94.7 us

profile of v5, /device:TPU:6, one launch (start us, length us, event | category | flops | bytes accessed | tf_op | source)
XLA Modules:
  0.0 96.8 jit_solution(1117830319462142725)
XLA Ops:
  0.6 94.7 %shard_map.118 = (bf16[160,1024]{1,0:T(8,128)(2,1)S(1)}, bf16[160,4608]{1,0:T(8,128)(2,1)S(1)}, bf16[1,288,1024]{2,1,0:T(8,128)(2,1)S(1)}, f32[1,4608]{1,0:T(1,1...) custom-call(bf16[160,4608]{1,0:T(8,128)(2,1)} %tok.1, f32[1,4608]{1,0:T(1,128)} %gain.1, bf16[1,288,1024]{2,1,0:T(8,128)(2,1)} %w.1, ...), custom_call_target="tpu_custom_call" | custom-call | flops 4529848320 | bytes 8388608 | tf_op jit(solution)/shard_map/pallas_call | solution.py:513
  95.3 1.5 %shard_map.119 = (bf16[160,1024]{1,0:T(8,128)(2,1)}, bf16[160,4608]{1,0:T(8,128)(2,1)}, bf16[1,288,1024]{2,1,0:T(8,128)(2,1)}, f32[1,4608]{1,0:T(1,128)}, f32[4,4608]{1,0:T(4,128)}, /*index=5*/f32[4,4608]{1,0:T(4,128)}) custom-call(bf16[160,1024]{1,0:T(8,128)(2,1)S(1)} %get-tuple-element.12.refs_0_, bf16[160,4608]{1,0:T(8,128)(2,1)S(1)} %get-tuple-element.13.refs_1_, ...), custom_call_target="tpu_custom_call" | custom-call | tf_op jit(solution)/shard_map/pallas_call | solution.py:576

commit v6 on v5

--- a/solution.py
+++ b/solution.py
@@ -92,16 +92,11 @@
     for member, earlier, peer, _ in pairs:
         pl.when(earlier & member)(functools.partial(greet, peer))
         greeted = greeted + jnp.where((~earlier) & member, 1, 0)
-    for copy in loads:
-        copy.start()
     pl.semaphore_wait(barrier, greeted)
 
     def tell(peer, sem):
         pl.semaphore_signal(sem, inc=1, device_id=peer, device_id_type=MESH)
 
-    pl.when(z > 0)(functools.partial(tell, below, above_in))
-    for member, earlier, peer, sem in pairs:
-        pl.when((~earlier) & member)(functools.partial(tell, peer, sem))
 
     def know(pair):
         member, earlier, _, sem = pair
@@ -132,6 +127,12 @@
     for j in (0, 1):
         for direction in (0, 1):
             ag_copy(direction, j).start()
+
+    for copy in loads:
+        copy.start()
+    pl.when(z > 0)(functools.partial(tell, below, above_in))
+    for member, earlier, peer, sem in pairs:
+        pl.when((~earlier) & member)(functools.partial(tell, peer, sem))
 
     x_c = remote(c2.at[pl.ds(0, ROWS)], c2.at[pl.ds(ROWS, ROWS)], x_ss.at[0], x_rs.at[0], partner)
     x_n = remote(nsend, n2.at[pl.ds(ROWS, ROWS)], x_ss.at[1], x_rs.at[1], partner)

time: 97.1 us -> 97 us (level)
  no operation moved by 1% of the time
where the time goes in v6:
time: 97 us; the launch traced here: 96.8 us
  Pallas kernels  96.2 us (99%)
    pallas_call x1, Pallas kernels, on_device(): pl.pallas_call(kernel, out_shape=[v(s.shape, s.dtype) for s in shapes], i...  94.7 us

profile of v6, /device:TPU:6, one launch (start us, length us, event | category | flops | bytes accessed | tf_op | source)
XLA Modules:
  0.0 96.8 jit_solution(17249328317464298495)
XLA Ops:
  0.6 94.7 %shard_map.118 = (bf16[160,1024]{1,0:T(8,128)(2,1)S(1)}, bf16[160,4608]{1,0:T(8,128)(2,1)S(1)}, bf16[1,288,1024]{2,1,0:T(8,128)(2,1)S(1)}, f32[1,4608]{1,0:T(1,1...) custom-call(bf16[160,4608]{1,0:T(8,128)(2,1)} %tok.1, f32[1,4608]{1,0:T(1,128)} %gain.1, bf16[1,288,1024]{2,1,0:T(8,128)(2,1)} %w.1, ...), custom_call_target="tpu_custom_call" | custom-call | flops 4529848320 | bytes 8388608 | tf_op jit(solution)/shard_map/pallas_call | solution.py:514
  95.3 1.5 %shard_map.119 = (bf16[160,1024]{1,0:T(8,128)(2,1)}, bf16[160,4608]{1,0:T(8,128)(2,1)}, bf16[1,288,1024]{2,1,0:T(8,128)(2,1)}, f32[1,4608]{1,0:T(1,128)}, f32[4,4608]{1,0:T(4,128)}, /*index=5*/f32[4,4608]{1,0:T(4,128)}) custom-call(bf16[160,1024]{1,0:T(8,128)(2,1)S(1)} %get-tuple-element.12.refs_0_, bf16[160,4608]{1,0:T(8,128)(2,1)S(1)} %get-tuple-element.13.refs_1_, ...), custom_call_target="tpu_custom_call" | custom-call | tf_op jit(solution)/shard_map/pallas_call | solution.py:577
